TPU v7x, 32 devices: a whole 2x2x4 slice. The times are simulated.
32 devices in a mesh: group: 2 (over y), comp: 4 (over z), sub: 4 (over x, core).
Axes of the slice: x: 2, y: 2, z: 4, core: 2. Of those that a mesh axis runs over, the one named last changes fastest.
Arguments:
- wind_u: bfloat16 [72, 131072], P(None, ('group', 'comp', 'sub')), parts along dimension 1, may hold values from 2 to 3
- wind_v: bfloat16 [72, 131072], P(None, ('group', 'comp', 'sub')), parts along dimension 1, may hold values from -3 to 3
- buoyancy_freq: bfloat16 [72, 131072], P(None, ('group', 'comp', 'sub')), parts along dimension 1, may hold values from 0.796875 to 1.25
- air_density: bfloat16 [72, 131072], P(None, ('group', 'comp', 'sub')), parts along dimension 1, may hold values from 0.0125 to 1.3
- layer_mass: bfloat16 [72, 131072], P(None, ('group', 'comp', 'sub')), parts along dimension 1, may hold values from 0.5 to 2
- orography: float32 [65536], P(('comp', 'sub')), may hold values from 0.2 to 1.5
- surface_flux: float32 [6, 131072], P(None, ('group', 'comp', 'sub')), parts along dimension 1, may hold values from -6 to 6
- send_list: int32 [16, 16, 2048], P(('comp', 'sub')), may hold values from 0 to 4095, as said below
- depth: float32 [512, 1024], P('comp', 'sub'), may hold values from 0.5 to 1.5
- ocean_state: float32 [5, 1024, 1024], P(None, ('group', 'comp'), 'sub'), parts along dimension 1, may hold values from -3 to 3
- map_slot: int32 [4, 512, 1024], P(None, 'comp', 'sub'), may hold values from 0 to 32767, as said below
- map_weight: float32 [4, 512, 1024], P(None, 'comp', 'sub'), may hold values from 0.1 to 0.5
Outputs:
- drag_tendency: bfloat16 [2, 72, 131072], P(None, None, ('group', 'comp', 'sub')), parts along dimension 2
- ocean_out: float32 [5, 1024, 1024], P(None, ('group', 'comp'), 'sub'), parts along dimension 1
There are 2 independent parts, one for each index of `group`. A program takes and returns all parts, laid end to end along the dimension named above; an argument that names none is the same for every part. Nothing has to cross between parts.
Inputs may be any that keep to these rules, and one draw needn't show every extreme that they name: Each entry names a column within the source device's block of 4096 columns; with q = d * 2048 + c, the entry send_list[s, d, c] lies in the block of 128 columns numbered (q // 128) % 32. `map_slot`: each entry names a slot that the cell's device receives, numbered source device times 2048 plus slot; for the cell at local row r and local column t of its device, with p = r * 256 + t, the slot lies in 128 * (p // 128) to 128 * (p // 128) + 127.
All inputs are finite; a program needn't handle non-finite values.
Results may differ from a plain program's by a relative error of at most 0.001.
Values sent between devices are 32-bit elements; how exact they have to be, the bound alone decides.
A program may use at most 64 MiB of HBM per device.

v0:
```python
import functools
import math

import jax
import jax.numpy as jnp
from jax import lax
from jax.experimental import pallas as pl
from jax.experimental.pallas import tpu as pltpu
from jax.sharding import PartitionSpec as P

SUBCYCLES = 8

SAT_SCALE = 0.1
BULK_SCALE = 0.2
TEND_SCALE = 8.0
WIND_PUSH = 0.1
HEAT_RATE = 0.2
SALT_RATE = 0.3
TIME_STEP = 0.6
BOTTOM_DRAG = 0.05
CORIOLIS_MAX = 0.2

LANES = 128
HALO = 2 * SUBCYCLES
GUARD = 8
TOP = GUARD + HALO
MESH = pl.DeviceIdType.MESH


def lane_gather(values, idx):
    return jnp.take_along_axis(values, idx, axis=1, mode="promise_in_bounds")


def gather_row_tile(values, idx):
    halves = [
        lane_gather(values[:, at : at + LANES], idx[:, at : at + LANES])
        for at in range(0, values.shape[1], LANES)
    ]
    return jnp.concatenate(halves, axis=1)


def kernel(
    n_comp,
    n_sub,
    wind_u,
    wind_v,
    buoyancy_freq,
    air_density,
    layer_mass,
    orography,
    surface_flux,
    send_list,
    depth,
    ocean_state,
    map_slot,
    map_weight,
    drag_hbm,
    ocean_hbm,
    wu,
    wv,
    bf,
    ad,
    lm,
    oro,
    flux,
    sends,
    slots,
    weights,
    tracers,
    drag,
    surface,
    fields,
    outgoing,
    received,
    state,
    push,
    cor,
    flux_n,
    height_x,
    pack_state,
    halo_state,
    pack_push,
    halo_push,
    in_sem,
    out_sem,
    a2a_send,
    a2a_recv,
    st_send,
    st_recv,
    pu_send,
    pu_recv,
):
    devices = n_comp * n_sub
    comp = lax.axis_index("comp")
    sub = lax.axis_index("sub")
    me = comp * n_sub + sub
    rows_dev, cols_dev = depth.shape
    per = sends.shape[1]
    dpt = 8 // per
    tiles = devices // dpt
    bottom = TOP + rows_dev
    levels, columns = wu.shape

    barrier = pltpu.get_barrier_semaphore()

    def greet(k, carry):
        d = lax.rem(me + k, devices)
        pl.semaphore_signal(
            barrier, inc=1, device_id={"comp": d // n_sub, "sub": lax.rem(d, n_sub)}, device_id_type=MESH
        )
        return carry

    lax.fori_loop(1, devices, greet, 0)

    loads = []

    def load(src, dst):
        copy = pltpu.make_async_copy(src, dst, in_sem.at[len(loads)])
        copy.start()
        loads.append(copy)
        return copy

    first = [
        load(wind_u, wu),
        load(wind_v, wv),
        load(buoyancy_freq, bf),
        load(air_density, ad),
        load(orography, oro),
        load(surface_flux, flux),
    ]
    first += [
        load(send_list.at[0, :, pl.ds(j * cols_dev, cols_dev)], sends.at[:, j]) for j in range(per)
    ]
    second = [
        load(ocean_state.at[0:3], state.at[0:3, pl.ds(TOP, rows_dev), pl.ds(0, cols_dev)]),
        load(depth, state.at[3, pl.ds(TOP, rows_dev), pl.ds(0, cols_dev)]),
    ]
    third = [load(layer_mass, lm)]
    fourth = [
        load(ocean_state.at[3:5], tracers),
        load(map_slot, slots),
        load(map_weight, weights),
    ]

    for guard in (0, bottom + HALO):
        state[:, guard : guard + GUARD, :] = jnp.zeros((4, GUARD, state.shape[2]), jnp.float32)
        flux_n[guard : guard + GUARD, :] = jnp.zeros((GUARD, state.shape[2]), jnp.float32)

    for copy in first:
        copy.wait()
    east = wu[0:1, :].astype(jnp.float32)
    north = wv[0:1, :].astype(jnp.float32)
    dens = ad[0:1, :].astype(jnp.float32)
    buoy = bf[0:1, :].astype(jnp.float32)
    height_sd = oro[0:1, :]
    speed = jnp.sqrt(east * east + north * north)
    inverse = 1.0 / speed
    dir_east = east * inverse
    dir_north = north * inverse
    base = dens * buoy * height_sd * height_sd * speed
    bulk = BULK_SCALE * dens * speed
    surface[0:1, :] = base
    surface[1:2, :] = TEND_SCALE * dir_east
    surface[2:3, :] = TEND_SCALE * dir_north
    sources = [
        base * dir_east + bulk * east,
        base * dir_north + bulk * north,
        flux[0:1, :] + flux[1:2, :] + flux[2:3, :] + flux[3:4, :],
        flux[4:5, :] - flux[5:6, :],
    ]
    field_rows = columns // cols_dev
    for f in range(4):
        for r in range(field_rows):
            fields[f, r : r + 1, :] = sources[f][:, r * cols_dev : (r + 1) * cols_dev]

    pl.semaphore_wait(barrier, devices - 1)

    def a2a_copy(d):
        return pltpu.make_async_remote_copy(
            src_ref=outgoing.at[d],
            dst_ref=received.at[me],
            send_sem=a2a_send.at[d],
            recv_sem=a2a_recv.at[me],
            device_id={"comp": d // n_sub, "sub": lax.rem(d, n_sub)},
            device_id_type=MESH,
        )

    def a2a_arrival(s):
        return pltpu.make_async_remote_copy(
            src_ref=outgoing.at[s],
            dst_ref=received.at[s],
            send_sem=a2a_send.at[s],
            recv_sem=a2a_recv.at[s],
            device_id={"comp": s // n_sub, "sub": lax.rem(s, n_sub)},
            device_id_type=MESH,
        )

    def pick(i, carry):
        tile = lax.rem(me // dpt + 1 + i, tiles)
        base_row = pl.multiple_of(lax.rem(tile, field_rows // 8) * 8, 8)
        idx = jnp.concatenate([sends[tile * dpt + j] for j in range(dpt)], axis=0) & (LANES - 1)
        for f in range(4):
            got = gather_row_tile(fields[f, pl.ds(base_row, 8), :], idx)
            for j in range(dpt):
                outgoing[tile * dpt + j, f] = got[j * per : (j + 1) * per]
        for j in range(dpt):
            d = tile * dpt + j

            @pl.when(d != me)
            def _():
                a2a_copy(d).start()

            @pl.when(d == me)
            def _():
                received[d] = outgoing[d]

        return carry

    lax.fori_loop(0, tiles, pick, 0)

    def halo_copies(cells, pack, halo, send_sem, recv_sem):
        up = lax.rem(comp + n_comp - 1, n_comp)
        down = lax.rem(comp + 1, n_comp)
        right = lax.rem(sub + 1, n_sub)
        left = lax.rem(sub + n_sub - 1, n_sub)
        wide = pl.ds(0, cols_dev)
        plan = [
            (
                cells.at[:, pl.ds(bottom - HALO, HALO), wide],
                cells.at[:, pl.ds(GUARD, HALO), wide],
                (down, sub),
            ),
            (
                cells.at[:, pl.ds(TOP, HALO), wide],
                cells.at[:, pl.ds(bottom, HALO), wide],
                (up, sub),
            ),
        ]
        for side, there in ((0, right), (1, left)):
            plan += [
                (pack.at[side], halo.at[side, pl.ds(HALO, rows_dev)], (comp, there)),
                (
                    pack.at[side, pl.ds(rows_dev - HALO, HALO)],
                    halo.at[side, pl.ds(0, HALO)],
                    (down, there),
                ),
                (
                    pack.at[side, pl.ds(0, HALO)],
                    halo.at[side, pl.ds(HALO + rows_dev, HALO)],
                    (up, there),
                ),
            ]
        return [
            pltpu.make_async_remote_copy(
                src_ref=src,
                dst_ref=dst,
                send_sem=send_sem.at[i],
                recv_sem=recv_sem.at[i],
                device_id={"comp": target[0], "sub": target[1]},
                device_id_type=MESH,
            )
            for i, (src, dst, target) in enumerate(plan)
        ]

    lane = lax.broadcasted_iota(jnp.int32, (rows_dev, LANES), 1)
    lane_halo = lax.broadcasted_iota(jnp.int32, (rows_dev + 2 * HALO, LANES), 1)

    def pack_edges(cells, count, pack):
        right_edge = cells[0, TOP:bottom, cols_dev - LANES : cols_dev]
        left_edge = cells[0, TOP:bottom, 0:LANES]
        for k in range(1, count):
            tile = cells[k, TOP:bottom, cols_dev - LANES : cols_dev]
            right_edge = jnp.where(
                lane < LANES - k * HALO, pltpu.roll(tile, LANES - k * HALO, 1), right_edge
            )
            tile = cells[k, TOP:bottom, 0:LANES]
            left_edge = jnp.where(lane >= k * HALO, pltpu.roll(tile, k * HALO, 1), left_edge)
        pack[0] = right_edge
        pack[1] = left_edge

    def unpack_edges(cells, count, halo):
        from_left = halo[0]
        from_right = halo[1]
        for k in range(count):
            left_k = pltpu.roll(from_left, k * HALO, 1) if k else from_left
            right_k = pltpu.roll(from_right, LANES - k * HALO, 1) if k else from_right
            cells[k, GUARD : bottom + HALO, cols_dev : cols_dev + LANES] = jnp.where(
                lane_halo < LANES // 2, right_k, left_k
            )

    for copy in second:
        copy.wait()
    pack_edges(state, 4, pack_state)
    state_copies = halo_copies(state, pack_state, halo_state, st_send, st_recv)
    for copy in state_copies:
        copy.start()

    total_rows = cor.shape[0]
    row_global = comp * rows_dev - TOP + lax.broadcasted_iota(jnp.int32, cor.shape, 0)
    phase = 2.0 * math.pi * (row_global.astype(jnp.float32) + 0.5) / (rows_dev * n_comp)
    cor[...] = (TIME_STEP * CORIOLIS_MAX) * jnp.cos(phase)

    for copy in third:
        copy.wait()
    width = 2 * LANES
    row8 = lax.broadcasted_iota(jnp.int32, (8, width), 0)

    def drag_chunk(c, carry):
        at = pl.ds(pl.multiple_of(c * width, width), width)
        u = wu[:, at].astype(jnp.float32)
        v = wv[:, at].astype(jnp.float32)
        sq = u * u + v * v
        sat = (
            SAT_SCALE
            * ad[:, at].astype(jnp.float32)
            * (sq * sq * lax.rsqrt(sq))
            / bf[:, at].astype(jnp.float32)
        )
        inv_mass = 1.0 / lm[:, at].astype(jnp.float32)
        above = jnp.broadcast_to(surface[0:1, at], (8, width))
        dir_e = jnp.broadcast_to(surface[1:2, at], (8, width))
        dir_n = jnp.broadcast_to(surface[2:3, at], (8, width))
        out_e = []
        out_n = []
        for lev in range(0, levels, 8):
            low = jnp.minimum(sat[lev : lev + 8], above)
            for shift in (1, 2, 4):
                low = jnp.minimum(low, jnp.where(row8 >= shift, pltpu.roll(low, shift, 0), low))
            below = jnp.where(row8 >= 1, pltpu.roll(low, 1, 0), above)
            change = (low - below) * inv_mass[lev : lev + 8]
            out_e.append(change * dir_e)
            out_n.append(change * dir_n)
            above = jnp.broadcast_to(low[7:8], (8, width))
        drag[0, :, at] = jnp.concatenate(out_e, axis=0).astype(jnp.bfloat16)
        drag[1, :, at] = jnp.concatenate(out_n, axis=0).astype(jnp.bfloat16)
        return carry

    lax.fori_loop(0, columns // width, drag_chunk, 0)
    drag_store = pltpu.make_async_copy(drag, drag_hbm, out_sem.at[0])
    drag_store.start()

    for copy in fourth:
        copy.wait()

    def spread(i, carry):
        tile = lax.rem(me // dpt + tiles - i, tiles)
        for j in range(dpt):
            s = tile * dpt + j

            @pl.when(s != me)
            def _():
                a2a_arrival(s).wait_recv()

        rows = pl.ds(pl.multiple_of(tile * 8, 8), 8)
        rows_in = pl.ds(pl.multiple_of(TOP + tile * 8, 8), 8)
        wide = pl.ds(0, cols_dev)
        idx = [slots[k, rows, :] & (LANES - 1) for k in range(slots.shape[0])]
        wgt = [weights[k, rows, :] for k in range(slots.shape[0])]
        forcing = []
        for f in range(4):
            values = jnp.concatenate([received[tile * dpt + j, f] for j in range(dpt)], axis=0)
            terms = [w * gather_row_tile(values, x) for w, x in zip(wgt, idx)]
            forcing.append(sum(terms[1:], terms[0]))
        scale = (TIME_STEP * WIND_PUSH) / state[3, rows_in, wide]
        push[0, rows_in, wide] = forcing[0] * scale
        push[1, rows_in, wide] = forcing[1] * scale
        tracers[0, rows, :] = tracers[0, rows, :] + HEAT_RATE * forcing[2]
        tracers[1, rows, :] = tracers[1, rows, :] - SALT_RATE * forcing[3]
        return carry

    lax.fori_loop(0, tiles, spread, 0)

    pack_edges(push, 2, pack_push)
    push_copies = halo_copies(push, pack_push, halo_push, pu_send, pu_recv)
    for copy in push_copies:
        copy.start()
    tracer_store = pltpu.make_async_copy(tracers, ocean_hbm.at[3:5], out_sem.at[1])
    tracer_store.start()
    for copy in state_copies:
        copy.wait_recv()
    unpack_edges(state, 4, halo_state)
    for copy in state_copies:
        copy.wait_send()
    for copy in push_copies:
        copy.wait()
    unpack_edges(push, 2, halo_push)

    span = state.shape[2]
    keep = 1.0 - TIME_STEP * BOTTOM_DRAG
    half = 0.5 * TIME_STEP
    chunk = 16
    copies = span // LANES

    def diff_east(a):
        return pltpu.roll(a, span - 1, 1) - pltpu.roll(a, 1, 1)

    def step(n, carry):
        for a in range(GUARD, bottom + HALO, chunk):
            h = state[0, a : a + chunk, :]
            u = state[1, a : a + chunk, :]
            v = state[2, a : a + chunk, :]
            d = state[3, a : a + chunk, :]
            turn = jnp.concatenate([cor[a : a + chunk, :]] * copies, axis=1)
            grad_n = state[0, a + 1 : a + chunk + 1, :] - state[0, a - 1 : a + chunk - 1, :]
            new_u = keep * u + turn * v - half * diff_east(h) + push[0, a : a + chunk, :]
            new_v = keep * v - turn * u - half * grad_n + push[1, a : a + chunk, :]
            state[1, a : a + chunk, :] = new_u
            state[2, a : a + chunk, :] = new_v
            flux_n[a : a + chunk, :] = d * new_v
            height_x[a : a + chunk, :] = h - half * diff_east(d * new_u)
        for a in range(GUARD, bottom + HALO, chunk):
            div_n = flux_n[a + 1 : a + chunk + 1, :] - flux_n[a - 1 : a + chunk - 1, :]
            state[0, a : a + chunk, :] = height_x[a : a + chunk, :] - half * div_n
        return carry

    lax.fori_loop(0, SUBCYCLES, step, 0)
    ocean_store = pltpu.make_async_copy(
        state.at[0:3, pl.ds(TOP, rows_dev), pl.ds(0, cols_dev)], ocean_hbm.at[0:3], out_sem.at[2]
    )
    ocean_store.start()

    def drain(k, carry):
        a2a_copy(lax.rem(me + k, devices)).wait_send()
        return carry

    lax.fori_loop(1, devices, drain, 0)
    drag_store.wait()
    tracer_store.wait()
    ocean_store.wait()


def shards(n_comp, n_sub, *args):
    wind_u, orography, surface_flux, send_list = args[0], args[5], args[6], args[7]
    depth, ocean_state, map_slot, map_weight = args[8:12]
    devices = n_comp * n_sub
    levels, columns = wind_u.shape
    rows_dev, cols_dev = depth.shape
    entries = map_slot.shape[0]
    cap = send_list.shape[2]
    per = cap // cols_dev
    total_rows = rows_dev + 2 * TOP
    span = cols_dev + LANES
    halo_rows = rows_dev + 2 * HALO
    f32 = jnp.float32
    air = pltpu.VMEM((levels, columns), jnp.bfloat16)
    args = args[:5] + (orography.reshape(1, -1),) + args[6:]
    dma = pltpu.SemaphoreType.DMA
    return pl.pallas_call(
        functools.partial(kernel, n_comp, n_sub),
        out_shape=(
            jax.ShapeDtypeStruct((2, levels, columns), jnp.bfloat16),
            jax.ShapeDtypeStruct(ocean_state.shape, f32),
        ),
        in_specs=[pl.BlockSpec(memory_space=pl.ANY)] * 12,
        out_specs=[pl.BlockSpec(memory_space=pl.ANY)] * 2,
        scratch_shapes=[
            air,
            air,
            air,
            air,
            air,
            pltpu.VMEM((1, columns), f32),
            pltpu.VMEM(surface_flux.shape, f32),
            pltpu.VMEM((devices, per, cols_dev), jnp.int32),
            pltpu.VMEM((entries, rows_dev, cols_dev), jnp.int32),
            pltpu.VMEM((entries, rows_dev, cols_dev), f32),
            pltpu.VMEM((2, rows_dev, cols_dev), f32),
            pltpu.VMEM((2, levels, columns), jnp.bfloat16),
            pltpu.VMEM((8, columns), f32),
            pltpu.VMEM((4, columns // cols_dev, cols_dev), f32),
            pltpu.VMEM((devices, 4, per, cols_dev), f32),
            pltpu.VMEM((devices, 4, per, cols_dev), f32),
            pltpu.VMEM((4, total_rows, span), f32),
            pltpu.VMEM((2, total_rows, span), f32),
            pltpu.VMEM((total_rows, LANES), f32),
            pltpu.VMEM((total_rows, span), f32),
            pltpu.VMEM((total_rows, span), f32),
            pltpu.VMEM((2, rows_dev, LANES), f32),
            pltpu.VMEM((2, halo_rows, LANES), f32),
            pltpu.VMEM((2, rows_dev, LANES), f32),
            pltpu.VMEM((2, halo_rows, LANES), f32),
            dma((12 + per,)),
            dma((3,)),
            dma((devices,)),
            dma((devices,)),
            dma((8,)),
            dma((8,)),
            dma((8,)),
            dma((8,)),
        ],
        compiler_params=pltpu.CompilerParams(
            collective_id=0, has_side_effects=True, vmem_limit_bytes=40 * 1024 * 1024
        ),
    )(*args)


def solution(mesh):
    return jax.shard_map(
        functools.partial(shards, mesh.shape["comp"], mesh.shape["sub"]),
        mesh=mesh,
        in_specs=(
            P(None, ("group", "comp", "sub")),
            P(None, ("group", "comp", "sub")),
            P(None, ("group", "comp", "sub")),
            P(None, ("group", "comp", "sub")),
            P(None, ("group", "comp", "sub")),
            P(("comp", "sub")),
            P(None, ("group", "comp", "sub")),
            P(("comp", "sub"), None, None),
            P("comp", "sub"),
            P(None, ("group", "comp"), "sub"),
            P(None, "comp", "sub"),
            P(None, "comp", "sub"),
        ),
        out_specs=(P(None, None, ("group", "comp", "sub")), P(None, ("group", "comp"), "sub")),
        check_vma=False,
    )
```

profile of v0, /device:TPU:0, one launch (start us, length us, event | category | flops | bytes accessed | tf_op | source)
XLA Modules:
  0.0 49.3 jit_solution(12844843592947426913)
XLA Ops:
  0.6 0.0 copy-start
  0.6 1.1 %copy-done = f32[5,128,256]{2,1,0:T(8,128)S(1)} copy-done((f32[5,128,256]{2,1,0:T(8,128)S(1)}, f32[5,128,256]{2,1,0:T(8,128)}, u32[]{:S(2)}) %copy-start) | copy-done | bytes 655384
  1.7 0.0 copy-start.1
  1.7 1.1 %copy-done.1 = bf16[72,4096]{1,0:T(8,128)(2,1)S(1)} copy-done((bf16[72,4096]{1,0:T(8,128)(2,1)S(1)}, bf16[72,4096]{1,0:T(8,128)(2,1)}, u32[]{:S(2)}) %copy-start.1) | copy-done | bytes 589848
  2.8 0.0 copy-start.2
  2.8 1.1 %copy-done.2 = bf16[72,4096]{1,0:T(8,128)(2,1)S(1)} copy-done((bf16[72,4096]{1,0:T(8,128)(2,1)S(1)}, bf16[72,4096]{1,0:T(8,128)(2,1)}, u32[]{:S(2)}) %copy-start.2) | copy-done | bytes 589848
  3.9 0.0 copy-start.3
  3.9 1.1 %copy-done.3 = bf16[72,4096]{1,0:T(8,128)(2,1)S(1)} copy-done((bf16[72,4096]{1,0:T(8,128)(2,1)S(1)}, bf16[72,4096]{1,0:T(8,128)(2,1)}, u32[]{:S(2)}) %copy-start.3) | copy-done | bytes 589848
  4.9 0.0 copy-start.4
  4.9 1.1 %copy-done.4 = bf16[72,4096]{1,0:T(8,128)(2,1)S(1)} copy-done((bf16[72,4096]{1,0:T(8,128)(2,1)S(1)}, bf16[72,4096]{1,0:T(8,128)(2,1)}, u32[]{:S(2)}) %copy-start.4) | copy-done | bytes 589848
  6.0 0.0 copy-start.5
  6.0 1.1 %copy-done.5 = bf16[72,4096]{1,0:T(8,128)(2,1)S(1)} copy-done((bf16[72,4096]{1,0:T(8,128)(2,1)S(1)}, bf16[72,4096]{1,0:T(8,128)(2,1)}, u32[]{:S(2)}) %copy-start.5) | copy-done | bytes 589848
  7.0 0.0 copy-start.6
  7.0 1.0 %copy-done.6 = s32[4,128,256]{2,1,0:T(8,128)S(1)} copy-done((s32[4,128,256]{2,1,0:T(8,128)S(1)}, s32[4,128,256]{2,1,0:T(8,128)}, u32[]{:S(2)}) %copy-start.6) | copy-done | bytes 524312
  8.1 0.0 copy-start.7
  8.1 1.0 %copy-done.7 = f32[4,128,256]{2,1,0:T(8,128)S(1)} copy-done((f32[4,128,256]{2,1,0:T(8,128)S(1)}, f32[4,128,256]{2,1,0:T(8,128)}, u32[]{:S(2)}) %copy-start.7) | copy-done | bytes 524312
  9.1 0.0 copy-start.8
  9.1 0.9 %copy-done.8 = f32[6,4096]{1,0:T(8,128)S(1)} copy-done((f32[6,4096]{1,0:T(8,128)S(1)}, f32[6,4096]{1,0:T(8,128)}, u32[]{:S(2)}) %copy-start.8) | copy-done | bytes 98328
  10.0 0.0 copy-start.9
  10.0 0.9 %copy-done.9 = s32[1,16,2048]{2,1,0:T(8,128)S(1)} copy-done((s32[1,16,2048]{2,1,0:T(8,128)S(1)}, s32[1,16,2048]{2,1,0:T(8,128)}, u32[]{:S(2)}) %copy-start.9) | copy-done | bytes 131096
  10.9 0.0 copy-start.10
  10.9 0.9 %copy-done.10 = f32[128,256]{1,0:T(8,128)S(1)} copy-done((f32[128,256]{1,0:T(8,128)S(1)}, f32[128,256]{1,0:T(8,128)}, u32[]{:S(2)}) %copy-start.10) | copy-done | bytes 131096
  11.8 0.0 copy-start.11
  11.8 0.7 %copy-done.11 = f32[4096]{0:T(1024)S(1)} copy-done((f32[4096]{0:T(1024)S(1)}, f32[4096]{0:T(1024)}, u32[]{:S(2)}) %copy-start.11) | copy-done | bytes 16408
  12.6 34.9 %shard_map.131 = (bf16[2,72,4096]{2,1,0:T(8,128)(2,1)S(1)}, f32[5,128,256]{2,1,0:T(8,128)S(1)}) custom-call(bf16[72,4096]{1,0:T(8,128)(2,1)S(1)} %copy-done.1, bf16[72,4096]{1,0:T(8,128)(2,1)S(1)} %copy-done.2, bf16[72,4096]{1,0:T(8,128)(2,1)S(1)} %copy-done.3, bf16[72,4096]{1,0:T(8,128)(2,1)S(1)} %copy-done.4, bf16[72,4096]{1,0:T(8,128)(2,1)S(1)} %copy-done.5, ...), custom_call_target="tpu_custom_call" | custom-call | tf_op jit(solution)/shard_map/pallas_call | solution.py:448
  47.4 1.0 %copy.16 = bf16[2,72,4096]{2,1,0:T(8,128)(2,1)} copy(bf16[2,72,4096]{2,1,0:T(8,128)(2,1)S(1)} %get-tuple-element.4) | data formatting | bytes 2359296
  48.5 0.8 %copy.17 = f32[5,128,256]{2,1,0:T(8,128)} copy(f32[5,128,256]{2,1,0:T(8,128)S(1)} %get-tuple-element.5) | data formatting | bytes 1310720
Async XLA Ops:
  0.6 1.1 %copy-start = (f32[5,128,256]{2,1,0:T(8,128)S(1)}, f32[5,128,256]{2,1,0:T(8,128)}, u32[]{:S(2)}) copy-start(f32[5,128,256]{2,1,0:T(8,128)} %ocean_state.1) | copy-start | bytes 1966084
  1.7 1.1 %copy-start.1 = (bf16[72,4096]{1,0:T(8,128)(2,1)S(1)}, bf16[72,4096]{1,0:T(8,128)(2,1)}, u32[]{:S(2)}) copy-start(bf16[72,4096]{1,0:T(8,128)(2,1)} %wind_u.1) | copy-start | bytes 1769476
  2.8 1.1 %copy-start.2 = (bf16[72,4096]{1,0:T(8,128)(2,1)S(1)}, bf16[72,4096]{1,0:T(8,128)(2,1)}, u32[]{:S(2)}) copy-start(bf16[72,4096]{1,0:T(8,128)(2,1)} %wind_v.1) | copy-start | bytes 1769476
  3.9 1.1 %copy-start.3 = (bf16[72,4096]{1,0:T(8,128)(2,1)S(1)}, bf16[72,4096]{1,0:T(8,128)(2,1)}, u32[]{:S(2)}) copy-start(bf16[72,4096]{1,0:T(8,128)(2,1)} %buoyancy_freq.1) | copy-start | bytes 1769476
  4.9 1.1 %copy-start.4 = (bf16[72,4096]{1,0:T(8,128)(2,1)S(1)}, bf16[72,4096]{1,0:T(8,128)(2,1)}, u32[]{:S(2)}) copy-start(bf16[72,4096]{1,0:T(8,128)(2,1)} %air_density.1) | copy-start | bytes 1769476
  6.0 1.1 %copy-start.5 = (bf16[72,4096]{1,0:T(8,128)(2,1)S(1)}, bf16[72,4096]{1,0:T(8,128)(2,1)}, u32[]{:S(2)}) copy-start(bf16[72,4096]{1,0:T(8,128)(2,1)} %layer_mass.1) | copy-start | bytes 1769476
  7.0 1.0 %copy-start.6 = (s32[4,128,256]{2,1,0:T(8,128)S(1)}, s32[4,128,256]{2,1,0:T(8,128)}, u32[]{:S(2)}) copy-start(s32[4,128,256]{2,1,0:T(8,128)} %map_slot.1) | copy-start | bytes 1572868
  8.1 1.0 %copy-start.7 = (f32[4,128,256]{2,1,0:T(8,128)S(1)}, f32[4,128,256]{2,1,0:T(8,128)}, u32[]{:S(2)}) copy-start(f32[4,128,256]{2,1,0:T(8,128)} %map_weight.1) | copy-start | bytes 1572868
  9.1 0.9 %copy-start.8 = (f32[6,4096]{1,0:T(8,128)S(1)}, f32[6,4096]{1,0:T(8,128)}, u32[]{:S(2)}) copy-start(f32[6,4096]{1,0:T(8,128)} %surface_flux.1) | copy-start | bytes 294916
  10.0 0.9 %copy-start.9 = (s32[1,16,2048]{2,1,0:T(8,128)S(1)}, s32[1,16,2048]{2,1,0:T(8,128)}, u32[]{:S(2)}) copy-start(s32[1,16,2048]{2,1,0:T(8,128)} %send_list.1) | copy-start | bytes 393220
  10.9 0.9 %copy-start.10 = (f32[128,256]{1,0:T(8,128)S(1)}, f32[128,256]{1,0:T(8,128)}, u32[]{:S(2)}) copy-start(f32[128,256]{1,0:T(8,128)} %depth.1) | copy-start | bytes 393220
  11.8 0.7 %copy-start.11 = (f32[4096]{0:T(1024)S(1)}, f32[4096]{0:T(1024)}, u32[]{:S(2)}) copy-start(f32[4096]{0:T(1024)} %param.17) | copy-start | bytes 49156
where the time goes:
time: 49.9 us; the launch traced here: 49.3 us
  Pallas kernels  34.9 us (70%)
  local copies, waits for them, and re-layouts  13.8 us (28%)
  between operations  0.66 us (1%)
    pallas_call x1, Pallas kernels, shards(): pl.pallas_call(functools.partial(kernel, n_comp, n_sub), out_shape=(jax.S...  34.9 us
    unnamed x26, local copies, waits for them, and re-layouts  13.8 us

commit v1 on v0

--- a/solution.py
+++ b/solution.py
@@ -120,6 +120,10 @@
         loads.append(copy)
         return copy
 
+    second = [
+        load(ocean_state.at[0:3], state.at[0:3, pl.ds(TOP, rows_dev), pl.ds(0, cols_dev)]),
+        load(depth, state.at[3, pl.ds(TOP, rows_dev), pl.ds(0, cols_dev)]),
+    ]
     first = [
         load(wind_u, wu),
         load(wind_v, wv),
@@ -131,10 +135,6 @@
     first += [
         load(send_list.at[0, :, pl.ds(j * cols_dev, cols_dev)], sends.at[:, j]) for j in range(per)
     ]
-    second = [
-        load(ocean_state.at[0:3], state.at[0:3, pl.ds(TOP, rows_dev), pl.ds(0, cols_dev)]),
-        load(depth, state.at[3, pl.ds(TOP, rows_dev), pl.ds(0, cols_dev)]),
-    ]
     third = [load(layer_mass, lm)]
     fourth = [
         load(ocean_state.at[3:5], tracers),
@@ -145,78 +145,6 @@
     for guard in (0, bottom + HALO):
         state[:, guard : guard + GUARD, :] = jnp.zeros((4, GUARD, state.shape[2]), jnp.float32)
         flux_n[guard : guard + GUARD, :] = jnp.zeros((GUARD, state.shape[2]), jnp.float32)
-
-    for copy in first:
-        copy.wait()
-    east = wu[0:1, :].astype(jnp.float32)
-    north = wv[0:1, :].astype(jnp.float32)
-    dens = ad[0:1, :].astype(jnp.float32)
-    buoy = bf[0:1, :].astype(jnp.float32)
-    height_sd = oro[0:1, :]
-    speed = jnp.sqrt(east * east + north * north)
-    inverse = 1.0 / speed
-    dir_east = east * inverse
-    dir_north = north * inverse
-    base = dens * buoy * height_sd * height_sd * speed
-    bulk = BULK_SCALE * dens * speed
-    surface[0:1, :] = base
-    surface[1:2, :] = TEND_SCALE * dir_east
-    surface[2:3, :] = TEND_SCALE * dir_north
-    sources = [
-        base * dir_east + bulk * east,
-        base * dir_north + bulk * north,
-        flux[0:1, :] + flux[1:2, :] + flux[2:3, :] + flux[3:4, :],
-        flux[4:5, :] - flux[5:6, :],
-    ]
-    field_rows = columns // cols_dev
-    for f in range(4):
-        for r in range(field_rows):
-            fields[f, r : r + 1, :] = sources[f][:, r * cols_dev : (r + 1) * cols_dev]
-
-    pl.semaphore_wait(barrier, devices - 1)
-
-    def a2a_copy(d):
-        return pltpu.make_async_remote_copy(
-            src_ref=outgoing.at[d],
-            dst_ref=received.at[me],
-            send_sem=a2a_send.at[d],
-            recv_sem=a2a_recv.at[me],
-            device_id={"comp": d // n_sub, "sub": lax.rem(d, n_sub)},
-            device_id_type=MESH,
-        )
-
-    def a2a_arrival(s):
-        return pltpu.make_async_remote_copy(
-            src_ref=outgoing.at[s],
-            dst_ref=received.at[s],
-            send_sem=a2a_send.at[s],
-            recv_sem=a2a_recv.at[s],
-            device_id={"comp": s // n_sub, "sub": lax.rem(s, n_sub)},
-            device_id_type=MESH,
-        )
-
-    def pick(i, carry):
-        tile = lax.rem(me // dpt + 1 + i, tiles)
-        base_row = pl.multiple_of(lax.rem(tile, field_rows // 8) * 8, 8)
-        idx = jnp.concatenate([sends[tile * dpt + j] for j in range(dpt)], axis=0) & (LANES - 1)
-        for f in range(4):
-            got = gather_row_tile(fields[f, pl.ds(base_row, 8), :], idx)
-            for j in range(dpt):
-                outgoing[tile * dpt + j, f] = got[j * per : (j + 1) * per]
-        for j in range(dpt):
-            d = tile * dpt + j
-
-            @pl.when(d != me)
-            def _():
-                a2a_copy(d).start()
-
-            @pl.when(d == me)
-            def _():
-                received[d] = outgoing[d]
-
-        return carry
-
-    lax.fori_loop(0, tiles, pick, 0)
 
     def halo_copies(cells, pack, halo, send_sem, recv_sem):
         up = lax.rem(comp + n_comp - 1, n_comp)
@@ -262,21 +190,22 @@
             for i, (src, dst, target) in enumerate(plan)
         ]
 
-    lane = lax.broadcasted_iota(jnp.int32, (rows_dev, LANES), 1)
     lane_halo = lax.broadcasted_iota(jnp.int32, (rows_dev + 2 * HALO, LANES), 1)
 
-    def pack_edges(cells, count, pack):
-        right_edge = cells[0, TOP:bottom, cols_dev - LANES : cols_dev]
-        left_edge = cells[0, TOP:bottom, 0:LANES]
+    def pack_edges(cells, count, pack, begin, end):
+        lane = lax.broadcasted_iota(jnp.int32, (end - begin, LANES), 1)
+        rows = slice(TOP + begin, TOP + end)
+        right_edge = cells[0, rows, cols_dev - LANES : cols_dev]
+        left_edge = cells[0, rows, 0:LANES]
         for k in range(1, count):
-            tile = cells[k, TOP:bottom, cols_dev - LANES : cols_dev]
+            tile = cells[k, rows, cols_dev - LANES : cols_dev]
             right_edge = jnp.where(
                 lane < LANES - k * HALO, pltpu.roll(tile, LANES - k * HALO, 1), right_edge
             )
-            tile = cells[k, TOP:bottom, 0:LANES]
+            tile = cells[k, rows, 0:LANES]
             left_edge = jnp.where(lane >= k * HALO, pltpu.roll(tile, k * HALO, 1), left_edge)
-        pack[0] = right_edge
-        pack[1] = left_edge
+        pack[0, begin:end] = right_edge
+        pack[1, begin:end] = left_edge
 
     def unpack_edges(cells, count, halo):
         from_left = halo[0]
@@ -290,10 +219,81 @@
 
     for copy in second:
         copy.wait()
-    pack_edges(state, 4, pack_state)
+    pack_edges(state, 4, pack_state, 0, rows_dev)
     state_copies = halo_copies(state, pack_state, halo_state, st_send, st_recv)
+    pl.semaphore_wait(barrier, devices - 1)
     for copy in state_copies:
         copy.start()
+
+    for copy in first:
+        copy.wait()
+    east = wu[0:1, :].astype(jnp.float32)
+    north = wv[0:1, :].astype(jnp.float32)
+    dens = ad[0:1, :].astype(jnp.float32)
+    buoy = bf[0:1, :].astype(jnp.float32)
+    height_sd = oro[0:1, :]
+    speed = jnp.sqrt(east * east + north * north)
+    inverse = 1.0 / speed
+    dir_east = east * inverse
+    dir_north = north * inverse
+    base = dens * buoy * height_sd * height_sd * speed
+    bulk = BULK_SCALE * dens * speed
+    surface[0:1, :] = base
+    surface[1:2, :] = TEND_SCALE * dir_east
+    surface[2:3, :] = TEND_SCALE * dir_north
+    sources = [
+        base * dir_east + bulk * east,
+        base * dir_north + bulk * north,
+        flux[0:1, :] + flux[1:2, :] + flux[2:3, :] + flux[3:4, :],
+        flux[4:5, :] - flux[5:6, :],
+    ]
+    field_rows = columns // cols_dev
+    for f in range(4):
+        for r in range(field_rows):
+            fields[f, r : r + 1, :] = sources[f][:, r * cols_dev : (r + 1) * cols_dev]
+
+    def a2a_copy(d):
+        return pltpu.make_async_remote_copy(
+            src_ref=outgoing.at[d],
+            dst_ref=received.at[me],
+            send_sem=a2a_send.at[d],
+            recv_sem=a2a_recv.at[me],
+            device_id={"comp": d // n_sub, "sub": lax.rem(d, n_sub)},
+            device_id_type=MESH,
+        )
+
+    def a2a_arrival(s):
+        return pltpu.make_async_remote_copy(
+            src_ref=outgoing.at[s],
+            dst_ref=received.at[s],
+            send_sem=a2a_send.at[s],
+            recv_sem=a2a_recv.at[s],
+            device_id={"comp": s // n_sub, "sub": lax.rem(s, n_sub)},
+            device_id_type=MESH,
+        )
+
+    def pick(i, carry):
+        tile = lax.rem(me // dpt + 1 + i, tiles)
+        base_row = pl.multiple_of(lax.rem(tile, field_rows // 8) * 8, 8)
+        idx = jnp.concatenate([sends[tile * dpt + j] for j in range(dpt)], axis=0) & (LANES - 1)
+        for f in range(4):
+            got = gather_row_tile(fields[f, pl.ds(base_row, 8), :], idx)
+            for j in range(dpt):
+                outgoing[tile * dpt + j, f] = got[j * per : (j + 1) * per]
+        for j in range(dpt):
+            d = tile * dpt + j
+
+            @pl.when(d != me)
+            def _():
+                a2a_copy(d).start()
+
+            @pl.when(d == me)
+            def _():
+                received[d] = outgoing[d]
+
+        return carry
+
+    lax.fori_loop(0, tiles, pick, 0)
 
     total_rows = cor.shape[0]
     row_global = comp * rows_dev - TOP + lax.broadcasted_iota(jnp.int32, cor.shape, 0)
@@ -342,8 +342,7 @@
     for copy in fourth:
         copy.wait()
 
-    def spread(i, carry):
-        tile = lax.rem(me // dpt + tiles - i, tiles)
+    def spread(tile):
         for j in range(dpt):
             s = tile * dpt + j
 
@@ -366,14 +365,28 @@
         push[1, rows_in, wide] = forcing[1] * scale
         tracers[0, rows, :] = tracers[0, rows, :] + HEAT_RATE * forcing[2]
         tracers[1, rows, :] = tracers[1, rows, :] - SALT_RATE * forcing[3]
-        return carry
-
-    lax.fori_loop(0, tiles, spread, 0)
-
-    pack_edges(push, 2, pack_push)
+
+    edge = HALO // 8
+    inner = tiles - 2 * edge
+
+    def spread_edge(i, carry):
+        spread(jnp.where(i < edge, i, i + inner))
+        return carry
+
+    def spread_inner(i, carry):
+        spread(edge + lax.rem(me // dpt + 2 * inner - i, inner))
+        return carry
+
     push_copies = halo_copies(push, pack_push, halo_push, pu_send, pu_recv)
-    for copy in push_copies:
-        copy.start()
+    lax.fori_loop(0, 2 * edge, spread_edge, 0)
+    pack_edges(push, 2, pack_push, 0, HALO)
+    pack_edges(push, 2, pack_push, rows_dev - HALO, rows_dev)
+    for i in (0, 1, 3, 4, 6, 7):
+        push_copies[i].start()
+    lax.fori_loop(0, inner, spread_inner, 0)
+    pack_edges(push, 2, pack_push, HALO, rows_dev - HALO)
+    for i in (2, 5):
+        push_copies[i].start()
     tracer_store = pltpu.make_async_copy(tracers, ocean_hbm.at[3:5], out_sem.at[1])
     tracer_store.start()
     for copy in state_copies:
@@ -448,11 +461,11 @@
     return pl.pallas_call(
         functools.partial(kernel, n_comp, n_sub),
         out_shape=(
-            jax.ShapeDtypeStruct((2, levels, columns), jnp.bfloat16),
+            pltpu.VMEM((2, levels, columns), jnp.bfloat16),
             jax.ShapeDtypeStruct(ocean_state.shape, f32),
         ),
-        in_specs=[pl.BlockSpec(memory_space=pl.ANY)] * 12,
-        out_specs=[pl.BlockSpec(memory_space=pl.ANY)] * 2,
+        in_specs=[pl.BlockSpec(memory_space=pltpu.HBM)] * 12,
+        out_specs=[pl.BlockSpec(memory_space=pltpu.HBM)] * 2,
         scratch_shapes=[
             air,
             air,
@@ -489,7 +502,7 @@
             dma((8,)),
         ],
         compiler_params=pltpu.CompilerParams(
-            collective_id=0, has_side_effects=True, vmem_limit_bytes=40 * 1024 * 1024
+            collective_id=0, has_side_effects=True, vmem_limit_bytes=58 * 1024 * 1024
         ),
     )(*args)
 

time: 49.9 us -> 37.6 us (0.75)
  local copies, waits for them, and re-layouts: 13.8 us -> 2.34 us
  Pallas kernels: 34.9 us -> 34.4 us
    unnamed x26 -> x4, local copies, waits for them, and re-layouts: 13.8 us -> 2.34 us
where the time goes in v1:
time: 37.6 us; the launch traced here: 37.4 us
  Pallas kernels  34.4 us (91%)
  local copies, waits for them, and re-layouts  2.34 us (6%)
  between operations  0.65 us (2%)
    pallas_call x1, Pallas kernels, shards(): pl.pallas_call(functools.partial(kernel, n_comp, n_sub), out_shape=(pltpu...  34.4 us
    unnamed x4, local copies, waits for them, and re-layouts  2.34 us

profile of v1, /device:TPU:0, one launch (start us, length us, event | category | flops | bytes accessed | tf_op | source)
XLA Modules:
  0.0 37.4 jit_solution(9910448318363199369)
XLA Ops:
  0.6 34.4 %shard_map.131 = (bf16[2,72,4096]{2,1,0:T(8,128)(2,1)S(1)}, f32[5,128,256]{2,1,0:T(8,128)}) custom-call(bf16[72,4096]{1,0:T(8,128)(2,1)} %wind_u.1, bf16[72,4096]{1,0:T(8,128)(2,1)} %wind_v.1, bf16[72,4096]{1,0:T(8,128)(2,1)} %buoyancy_freq.1, bf16[72,4096]{1,0:T(8,128)(2,1)} %air_density.1, bf16[72,4096]{1,0:T(8,128)(2,1)} %layer_mass.1, ...), custom_call_target="tpu_custom_call" | custom-call | tf_op jit(solution)/shard_map/pallas_call | solution.py:461
  35.1 0.0 copy-start
  35.1 1.0 %copy.16 = bf16[2,72,4096]{2,1,0:T(8,128)(2,1)} copy(bf16[2,72,4096]{2,1,0:T(8,128)(2,1)S(1)} %get-tuple-element.2) | data formatting | bytes 2359296
  36.1 0.5 %copy-done = f32[5,128,256]{2,1,0:T(8,128)S(1)} copy-done((f32[5,128,256]{2,1,0:T(8,128)S(1)}, f32[5,128,256]{2,1,0:T(8,128)}, u32[]{:S(2)}) %copy-start) | copy-done | bytes 655384
  36.6 0.8 %copy.17 = f32[5,128,256]{2,1,0:T(8,128)} copy(f32[5,128,256]{2,1,0:T(8,128)S(1)} %copy-done) | data formatting | bytes 1310720
Async XLA Ops:
  35.1 1.5 %copy-start = (f32[5,128,256]{2,1,0:T(8,128)S(1)}, f32[5,128,256]{2,1,0:T(8,128)}, u32[]{:S(2)}) copy-start(f32[5,128,256]{2,1,0:T(8,128)} %get-tuple-element.7) | copy-start | bytes 1966084

commit v2 on v1

--- a/solution.py
+++ b/solution.py
@@ -70,7 +70,8 @@
     drag,
     surface,
     fields,
-    outgoing,
+    tables,
+    stage,
     received,
     state,
     push,
@@ -83,6 +84,10 @@
     halo_push,
     in_sem,
     out_sem,
+    ix_send,
+    ix_recv,
+    z_send,
+    z_recv,
     a2a_send,
     a2a_recv,
     st_send,
@@ -221,11 +226,7 @@
         copy.wait()
     pack_edges(state, 4, pack_state, 0, rows_dev)
     state_copies = halo_copies(state, pack_state, halo_state, st_send, st_recv)
-    pl.semaphore_wait(barrier, devices - 1)
-    for copy in state_copies:
-        copy.start()
-
-    for copy in first:
+    for copy in first[:6]:
         copy.wait()
     east = wu[0:1, :].astype(jnp.float32)
     north = wv[0:1, :].astype(jnp.float32)
@@ -250,50 +251,72 @@
     field_rows = columns // cols_dev
     for f in range(4):
         for r in range(field_rows):
-            fields[f, r : r + 1, :] = sources[f][:, r * cols_dev : (r + 1) * cols_dev]
-
-    def a2a_copy(d):
+            fields[r // per, f, r % per : r % per + 1, :] = sources[f][:, r * cols_dev : (r + 1) * cols_dev]
+
+    for copy in first[6:]:
+        copy.wait()
+    pl.semaphore_wait(barrier, devices - 1)
+
+    def place(d):
+        return {"comp": d // n_sub, "sub": lax.rem(d, n_sub)}
+
+    def list_copy(d, at):
         return pltpu.make_async_remote_copy(
-            src_ref=outgoing.at[d],
-            dst_ref=received.at[me],
-            send_sem=a2a_send.at[d],
-            recv_sem=a2a_recv.at[me],
-            device_id={"comp": d // n_sub, "sub": lax.rem(d, n_sub)},
+            src_ref=sends.at[d],
+            dst_ref=tables.at[at],
+            send_sem=ix_send.at[d],
+            recv_sem=ix_recv.at[at],
+            device_id=place(d),
             device_id_type=MESH,
         )
 
-    def a2a_arrival(s):
+    def send_lists(k, carry):
+        list_copy(lax.rem(me + k, devices), me).start()
+        return carry
+
+
+    blocks = fields.shape[0]
+    union = stage.shape[1]
+
+    def comp_copy(there, at):
+        begin = lax.rem(there * n_sub, blocks)
         return pltpu.make_async_remote_copy(
-            src_ref=outgoing.at[s],
-            dst_ref=received.at[s],
-            send_sem=a2a_send.at[s],
-            recv_sem=a2a_recv.at[s],
-            device_id={"comp": s // n_sub, "sub": lax.rem(s, n_sub)},
+            src_ref=fields.at[pl.ds(begin, union)],
+            dst_ref=stage.at[at],
+            send_sem=z_send.at[there],
+            recv_sem=z_recv.at[at],
+            device_id={"comp": there, "sub": sub},
             device_id_type=MESH,
         )
 
-    def pick(i, carry):
-        tile = lax.rem(me // dpt + 1 + i, tiles)
-        base_row = pl.multiple_of(lax.rem(tile, field_rows // 8) * 8, 8)
-        idx = jnp.concatenate([sends[tile * dpt + j] for j in range(dpt)], axis=0) & (LANES - 1)
-        for f in range(4):
-            got = gather_row_tile(fields[f, pl.ds(base_row, 8), :], idx)
-            for j in range(dpt):
-                outgoing[tile * dpt + j, f] = got[j * per : (j + 1) * per]
-        for j in range(dpt):
-            d = tile * dpt + j
-
-            @pl.when(d != me)
-            def _():
-                a2a_copy(d).start()
-
-            @pl.when(d == me)
-            def _():
-                received[d] = outgoing[d]
-
-        return carry
-
-    lax.fori_loop(0, tiles, pick, 0)
+    def sub_copy(z, there, at):
+        return pltpu.make_async_remote_copy(
+            src_ref=stage.at[z, lax.rem(there, union)],
+            dst_ref=received.at[z * n_sub + at],
+            send_sem=a2a_send.at[z * n_sub + there],
+            recv_sem=a2a_recv.at[z * n_sub + at],
+            device_id={"comp": comp, "sub": there},
+            device_id_type=MESH,
+        )
+
+    def send_comp(k, carry):
+        there = lax.rem(comp + n_comp - k, n_comp)
+        comp_copy(there, comp).start()
+        return carry
+
+    lax.fori_loop(1, n_comp, send_comp, 0)
+    lax.fori_loop(1, devices, send_lists, 0)
+    tables[me] = sends[me]
+    stage[comp] = fields[pl.ds(lax.rem(comp * n_sub, blocks), union)]
+
+    def hand_on(z):
+        for k in range(1, n_sub):
+            sub_copy(z, lax.rem(sub + k, n_sub), sub).start()
+        received[z * n_sub + sub] = stage[z, lax.rem(sub, union)]
+
+    hand_on(comp)
+    for copy in state_copies:
+        copy.start()
 
     total_rows = cor.shape[0]
     row_global = comp * rows_dev - TOP + lax.broadcasted_iota(jnp.int32, cor.shape, 0)
@@ -339,21 +362,45 @@
     drag_store = pltpu.make_async_copy(drag, drag_hbm, out_sem.at[0])
     drag_store.start()
 
+    def pass_on(k, carry):
+        z = lax.rem(comp + k, n_comp)
+        comp_copy(z, z).wait_recv()
+        hand_on(z)
+        return carry
+
+    lax.fori_loop(1, n_comp, pass_on, 0)
+
     for copy in fourth:
         copy.wait()
+
+    def join(tile, carry):
+        for j in range(dpt):
+            s = tile * dpt + j
+
+            @pl.when(s != me)
+            def _():
+                list_copy(s, s).wait_recv()
+
+        rows = pl.ds(pl.multiple_of(tile * 8, 8), 8)
+        table = jnp.concatenate([tables[tile * dpt + j] for j in range(dpt)], axis=0) & (LANES - 1)
+        for k in range(slots.shape[0]):
+            slots[k, rows, :] = gather_row_tile(table, slots[k, rows, :] & (LANES - 1))
+        return carry
+
+    lax.fori_loop(0, tiles, join, 0)
 
     def spread(tile):
         for j in range(dpt):
             s = tile * dpt + j
 
-            @pl.when(s != me)
+            @pl.when(lax.rem(s, n_sub) != sub)
             def _():
-                a2a_arrival(s).wait_recv()
+                sub_copy(s // n_sub, lax.rem(s, n_sub), lax.rem(s, n_sub)).wait_recv()
 
         rows = pl.ds(pl.multiple_of(tile * 8, 8), 8)
         rows_in = pl.ds(pl.multiple_of(TOP + tile * 8, 8), 8)
         wide = pl.ds(0, cols_dev)
-        idx = [slots[k, rows, :] & (LANES - 1) for k in range(slots.shape[0])]
+        idx = [slots[k, rows, :] for k in range(slots.shape[0])]
         wgt = [weights[k, rows, :] for k in range(slots.shape[0])]
         forcing = []
         for f in range(4):
@@ -401,14 +448,14 @@
     span = state.shape[2]
     keep = 1.0 - TIME_STEP * BOTTOM_DRAG
     half = 0.5 * TIME_STEP
-    chunk = 16
     copies = span // LANES
 
     def diff_east(a):
         return pltpu.roll(a, span - 1, 1) - pltpu.roll(a, 1, 1)
 
-    def step(n, carry):
-        for a in range(GUARD, bottom + HALO, chunk):
+    def step(margin, n, carry):
+        chunk = rows_dev // 2 + margin
+        for a in range(TOP - margin, bottom + margin, chunk):
             h = state[0, a : a + chunk, :]
             u = state[1, a : a + chunk, :]
             v = state[2, a : a + chunk, :]
@@ -421,20 +468,33 @@
             state[2, a : a + chunk, :] = new_v
             flux_n[a : a + chunk, :] = d * new_v
             height_x[a : a + chunk, :] = h - half * diff_east(d * new_u)
-        for a in range(GUARD, bottom + HALO, chunk):
+        for a in range(TOP - margin, bottom + margin, chunk):
             div_n = flux_n[a + 1 : a + chunk + 1, :] - flux_n[a - 1 : a + chunk - 1, :]
             state[0, a : a + chunk, :] = height_x[a : a + chunk, :] - half * div_n
         return carry
 
-    lax.fori_loop(0, SUBCYCLES, step, 0)
+    lax.fori_loop(0, SUBCYCLES // 2, functools.partial(step, HALO), 0)
+    lax.fori_loop(SUBCYCLES // 2, SUBCYCLES, functools.partial(step, HALO // 2), 0)
     ocean_store = pltpu.make_async_copy(
         state.at[0:3, pl.ds(TOP, rows_dev), pl.ds(0, cols_dev)], ocean_hbm.at[0:3], out_sem.at[2]
     )
     ocean_store.start()
 
     def drain(k, carry):
-        a2a_copy(lax.rem(me + k, devices)).wait_send()
-        return carry
+        list_copy(lax.rem(me + k, devices), me).wait_send()
+        return carry
+
+    def drain_comp(k, carry):
+        comp_copy(lax.rem(comp + k, n_comp), comp).wait_send()
+        return carry
+
+    def drain_sub(z, carry):
+        for k in range(1, n_sub):
+            sub_copy(z, lax.rem(sub + k, n_sub), sub).wait_send()
+        return carry
+
+    lax.fori_loop(1, n_comp, drain_comp, 0)
+    lax.fori_loop(0, n_comp, drain_sub, 0)
 
     lax.fori_loop(1, devices, drain, 0)
     drag_store.wait()
@@ -451,6 +511,7 @@
     entries = map_slot.shape[0]
     cap = send_list.shape[2]
     per = cap // cols_dev
+    blocks = columns // (cols_dev * per)
     total_rows = rows_dev + 2 * TOP
     span = cols_dev + LANES
     halo_rows = rows_dev + 2 * HALO
@@ -480,8 +541,9 @@
             pltpu.VMEM((2, rows_dev, cols_dev), f32),
             pltpu.VMEM((2, levels, columns), jnp.bfloat16),
             pltpu.VMEM((8, columns), f32),
-            pltpu.VMEM((4, columns // cols_dev, cols_dev), f32),
-            pltpu.VMEM((devices, 4, per, cols_dev), f32),
+            pltpu.VMEM((blocks, 4, per, cols_dev), f32),
+            pltpu.VMEM((devices, per, cols_dev), jnp.int32),
+            pltpu.VMEM((n_comp, min(blocks, n_sub), 4, per, cols_dev), f32),
             pltpu.VMEM((devices, 4, per, cols_dev), f32),
             pltpu.VMEM((4, total_rows, span), f32),
             pltpu.VMEM((2, total_rows, span), f32),
@@ -494,6 +556,10 @@
             pltpu.VMEM((2, halo_rows, LANES), f32),
             dma((12 + per,)),
             dma((3,)),
+            dma((devices,)),
+            dma((devices,)),
+            dma((n_comp,)),
+            dma((n_comp,)),
             dma((devices,)),
             dma((devices,)),
             dma((8,)),

time: 37.6 us -> 34.4 us (0.915)
  Pallas kernels: 34.4 us -> 31.1 us
    pallas_call x1, Pallas kernels: 34.4 us -> 31.1 us  [shards(): pl.pallas_call(functools.partial(kernel, n_comp, n_sub), out_shape=(pltpu...]
where the time goes in v2:
time: 34.4 us; the launch traced here: 34.1 us
  Pallas kernels  31.1 us (90%)
  local copies, waits for them, and re-layouts  2.34 us (7%)
  between operations  0.65 us (2%)
    pallas_call x1, Pallas kernels, shards(): pl.pallas_call(functools.partial(kernel, n_comp, n_sub), out_shape=(pltpu...  31.1 us
    unnamed x4, local copies, waits for them, and re-layouts  2.34 us

profile of v2, /device:TPU:0, one launch (start us, length us, event | category | flops | bytes accessed | tf_op | source)
XLA Modules:
  0.0 34.1 jit_solution(643866220138524797)
XLA Ops:
  0.6 31.1 %shard_map.131 = (bf16[2,72,4096]{2,1,0:T(8,128)(2,1)S(1)}, f32[5,128,256]{2,1,0:T(8,128)}) custom-call(bf16[72,4096]{1,0:T(8,128)(2,1)} %wind_u.1, bf16[72,4096]{1,0:T(8,128)(2,1)} %wind_v.1, bf16[72,4096]{1,0:T(8,128)(2,1)} %buoyancy_freq.1, bf16[72,4096]{1,0:T(8,128)(2,1)} %air_density.1, bf16[72,4096]{1,0:T(8,128)(2,1)} %layer_mass.1, ...), custom_call_target="tpu_custom_call" | custom-call | tf_op jit(solution)/shard_map/pallas_call | solution.py:522
  31.8 0.0 copy-start
  31.8 1.0 %copy.16 = bf16[2,72,4096]{2,1,0:T(8,128)(2,1)} copy(bf16[2,72,4096]{2,1,0:T(8,128)(2,1)S(1)} %get-tuple-element.2) | data formatting | bytes 2359296
  32.8 0.5 %copy-done = f32[5,128,256]{2,1,0:T(8,128)S(1)} copy-done((f32[5,128,256]{2,1,0:T(8,128)S(1)}, f32[5,128,256]{2,1,0:T(8,128)}, u32[]{:S(2)}) %copy-start) | copy-done | bytes 655384
  33.3 0.8 %copy.17 = f32[5,128,256]{2,1,0:T(8,128)} copy(f32[5,128,256]{2,1,0:T(8,128)S(1)} %copy-done) | data formatting | bytes 1310720
Async XLA Ops:
  31.8 1.5 %copy-start = (f32[5,128,256]{2,1,0:T(8,128)S(1)}, f32[5,128,256]{2,1,0:T(8,128)}, u32[]{:S(2)}) copy-start(f32[5,128,256]{2,1,0:T(8,128)} %get-tuple-element.7) | copy-start | bytes 1966084

commit v3 on v2

--- a/solution.py
+++ b/solution.py
@@ -315,8 +315,6 @@
         received[z * n_sub + sub] = stage[z, lax.rem(sub, union)]
 
     hand_on(comp)
-    for copy in state_copies:
-        copy.start()
 
     total_rows = cor.shape[0]
     row_global = comp * rows_dev - TOP + lax.broadcasted_iota(jnp.int32, cor.shape, 0)
@@ -358,10 +356,7 @@
         drag[1, :, at] = jnp.concatenate(out_n, axis=0).astype(jnp.bfloat16)
         return carry
 
-    lax.fori_loop(0, columns // width, drag_chunk, 0)
-    drag_store = pltpu.make_async_copy(drag, drag_hbm, out_sem.at[0])
-    drag_store.start()
-
+    lax.fori_loop(0, columns // width // 2, drag_chunk, 0)
     def pass_on(k, carry):
         z = lax.rem(comp + k, n_comp)
         comp_copy(z, z).wait_recv()
@@ -369,6 +364,11 @@
         return carry
 
     lax.fori_loop(1, n_comp, pass_on, 0)
+    for copy in state_copies:
+        copy.start()
+    lax.fori_loop(columns // width // 2, columns // width, drag_chunk, 0)
+    drag_store = pltpu.make_async_copy(drag, drag_hbm, out_sem.at[0])
+    drag_store.start()
 
     for copy in fourth:
         copy.wait()

time: 34.4 us -> 33.5 us (0.974)
  Pallas kernels: 31.1 us -> 30.3 us
    pallas_call x1, Pallas kernels: 31.1 us -> 30.3 us  [shards(): pl.pallas_call(functools.partial(kernel, n_comp, n_sub), out_shape=(pltpu...]
where the time goes in v3:
time: 33.5 us; the launch traced here: 33.3 us
  Pallas kernels  30.3 us (90%)
  local copies, waits for them, and re-layouts  2.34 us (7%)
  between operations  0.65 us (2%)
    pallas_call x1, Pallas kernels, shards(): pl.pallas_call(functools.partial(kernel, n_comp, n_sub), out_shape=(pltpu...  30.3 us
    unnamed x4, local copies, waits for them, and re-layouts  2.34 us

profile of v3, /device:TPU:0, one launch (start us, length us, event | category | flops | bytes accessed | tf_op | source)
XLA Modules:
  0.0 33.3 jit_solution(7214765799420803705)
XLA Ops:
  0.6 30.3 %shard_map.131 = (bf16[2,72,4096]{2,1,0:T(8,128)(2,1)S(1)}, f32[5,128,256]{2,1,0:T(8,128)}) custom-call(bf16[72,4096]{1,0:T(8,128)(2,1)} %wind_u.1, bf16[72,4096]{1,0:T(8,128)(2,1)} %wind_v.1, bf16[72,4096]{1,0:T(8,128)(2,1)} %buoyancy_freq.1, bf16[72,4096]{1,0:T(8,128)(2,1)} %air_density.1, bf16[72,4096]{1,0:T(8,128)(2,1)} %layer_mass.1, ...), custom_call_target="tpu_custom_call" | custom-call | tf_op jit(solution)/shard_map/pallas_call | solution.py:522
  30.9 0.0 copy-start
  30.9 1.0 %copy.16 = bf16[2,72,4096]{2,1,0:T(8,128)(2,1)} copy(bf16[2,72,4096]{2,1,0:T(8,128)(2,1)S(1)} %get-tuple-element.2) | data formatting | bytes 2359296
  31.9 0.5 %copy-done = f32[5,128,256]{2,1,0:T(8,128)S(1)} copy-done((f32[5,128,256]{2,1,0:T(8,128)S(1)}, f32[5,128,256]{2,1,0:T(8,128)}, u32[]{:S(2)}) %copy-start) | copy-done | bytes 655384
  32.4 0.8 %copy.17 = f32[5,128,256]{2,1,0:T(8,128)} copy(f32[5,128,256]{2,1,0:T(8,128)S(1)} %copy-done) | data formatting | bytes 1310720
Async XLA Ops:
  30.9 1.5 %copy-start = (f32[5,128,256]{2,1,0:T(8,128)S(1)}, f32[5,128,256]{2,1,0:T(8,128)}, u32[]{:S(2)}) copy-start(f32[5,128,256]{2,1,0:T(8,128)} %get-tuple-element.7) | copy-start | bytes 1966084
